TPU v7x, 32 devices: a whole 2x2x4 slice. The times are simulated.
32 devices in a mesh: ctx: 16 (over z, x, core), head: 2 (over y).
Axes of the slice: x: 2, y: 2, z: 4, core: 2. Of those that a mesh axis runs over, the one named last changes fastest.
Arguments:
- x_in: bfloat16 [4096, 5120], P('ctx', 'head'), may hold values from -6 to 6
- z_in: bfloat16 [4096, 5120], P('ctx', 'head'), may hold values from -48 to 48
- bc_in: bfloat16 [256, 4096], P('head', 'ctx'), may hold values from -6 to 6
- dt_in: float32 [80, 4096], P('head', 'ctx'), may hold values from -1 to 1
- dt_bias: float32 [80], P('head'), may hold values from -6 to 1
- decay_rate: float32 [80], P('head'), may hold values from 0 to 1, as said below
- d_skip: float32 [80], P('head'), may hold values from 1 to 6
- conv_x: float32 [4, 5120], P(None, 'head'), may hold values from -3 to 3
- conv_bc: float32 [256, 4], replicated, may hold values from -3 to 3
- norm_gain: float32 [5120], P('head'), may hold values from 0.1 to 1.9
- w_out: bfloat16 [5120, 2560], P('head'), may hold values from -0.125 to 0.125
Outputs:
- layer_out: bfloat16 [2560, 4096], P('head', 'ctx')
Inputs may be any that keep to these rules, and one draw needn't show every extreme that they name: `decay_rate`: each head's decay rate is positive.
All inputs are finite; a program needn't handle non-finite values.
Results may differ from a plain program's by a relative error of at most 0.019.
Values may be sent and summed in bfloat16 or wider, within the bound.
A program may use at most 128 MiB of HBM per device.

v0:
```python
import functools

import jax
import jax.numpy as jnp
from jax import lax
from jax.experimental import pallas as pl
from jax.experimental.pallas import tpu as pltpu
from jax.sharding import PartitionSpec as P

HEADS = 80
N = 128
P_SIZE = 64
KCONV = 4
SPAN = 256


EPSILON = 1e-05
MESH = pl.DeviceIdType.MESH


def from_behind(value, axis, steps):
    count = lax.axis_size(axis)
    first, last = (max(0, -steps), min(count, count - steps))
    return lax.ppermute(value, axis, [(source, source + steps) for source in range(first, last)])


STEPS = 5
CHUNK = 256


def silu(v):
    return v / (1.0 + jnp.exp(-v))


def mixer_kernel(
    groups, chunks, s_ref, k_ref, xc_ref, score_ref, cum_ref, delta_ref, c_ref, skip_ref, gain_ref,
    z_ref, w_ref, *rest,
):
    if chunks:
        own_ref, got_ref, inv_ref, *rest = rest
        w_s, send_s, sq_s, sq_own, hid_s, load, psend, precv, sq_sem, *rest = rest
    else:
        hid_s, sq_own, *rest = rest
    (
        z_s, z_sem, y_s, e_s, ra, rka, tb, ktb, rb, rkb, sc, rc, sd, rd, oe, se,
        send, recv, ksend, krecv,
    ) = rest
    f32, bf16 = jnp.float32, jnp.bfloat16
    idx = lax.axis_index("ctx")
    hd = lax.axis_index("head")
    c = lax.rem(idx, 2)
    x = lax.rem(lax.div(idx, 2), 2)
    g = lax.div(idx, 4)
    core_peer = idx + 1 - 2 * c
    x_peer = idx + 2 - 4 * x
    has_prev = g > 0
    has_next = g < groups - 1
    heads = k_ref.shape[0]
    size = heads // STEPS
    cols = size * P_SIZE
    length = xc_ref.shape[0]

    barrier = pltpu.get_barrier_semaphore()
    pl.semaphore_signal(barrier, inc=1, device_id=(core_peer, hd), device_id_type=MESH)
    pl.semaphore_signal(barrier, inc=1, device_id=(x_peer, hd), device_id_type=MESH)
    if chunks:
        pl.semaphore_signal(barrier, inc=1, device_id=(idx, 1 - hd), device_id_type=MESH)

    @pl.when(has_prev)
    def _():
        pl.semaphore_signal(barrier, inc=1, device_id=(idx - 4, hd), device_id_type=MESH)

    @pl.when(has_next)
    def _():
        pl.semaphore_signal(barrier, inc=1, device_id=(idx + 4, hd), device_id_type=MESH)

    z_load = pltpu.make_async_copy(z_ref, z_s, z_sem.at[0])
    z_load.start()
    loads = []
    for i in range(2 * chunks):
        base = (1 - hd if i < chunks else hd) * (chunks * CHUNK) + (i % chunks) * CHUNK
        base = pl.multiple_of(base, CHUNK)
        cp = pltpu.make_async_copy(w_ref.at[:, pl.ds(base, CHUNK)], w_s.at[i], load.at[i])
        cp.start()
        loads.append(cp)

    greeted = 3 if chunks else 2
    pl.semaphore_wait(barrier, greeted + has_prev.astype(jnp.int32) + has_next.astype(jnp.int32))

    def copy(src, dst, phase, j, dev):
        return pltpu.make_async_remote_copy(
            src_ref=src, dst_ref=dst, send_sem=send.at[phase, j], recv_sem=recv.at[phase, j],
            device_id=(dev, hd), device_id_type=MESH,
        )

    def keep_copy(src, dst, j, dev):
        return pltpu.make_async_remote_copy(
            src_ref=src, dst_ref=dst, send_sem=ksend.at[j], recv_sem=krecv.at[j],
            device_id=(dev, hd), device_id_type=MESH,
        )

    part = [pl.ds(j * size, size) for j in range(STEPS)]
    ka = keep_copy(k_ref, rka, 0, core_peer)
    ka.start()
    step_a = [copy(s_ref.at[1 - c, :, d], ra.at[:, d], 0, j, core_peer) for j, d in enumerate(part)]
    for cp in step_a:
        cp.start()

    @pl.when(jnp.logical_not(has_prev))
    def _():
        rc[...] = jnp.zeros_like(rc)

    def local_chunks(low, high):
        @pl.loop(low, high)
        def _(i):
            cum8 = cum_ref[i]
            delta8 = delta_ref[i]
            cum_cols = cum8.T
            scores = score_ref[...]
            left = lax.broadcasted_iota(jnp.int32, (length, 128), 1) < P_SIZE
            for j in range(size // 2):
                lanes = pl.ds(pl.multiple_of(i * cols + j * 128, 128), 128)
                pair = xc_ref[:, lanes].astype(f32)
                weights = []
                for h in (2 * j, 2 * j + 1):
                    gap = jnp.minimum(cum_cols[:, h : h + 1] - cum8[h : h + 1], 0.0)
                    weights.append((scores * jnp.exp(gap) * delta8[h : h + 1]).astype(bf16))
                both = jnp.concatenate(
                    [jnp.where(left, pair, 0.0), jnp.where(left, 0.0, pair)], 0
                ).astype(bf16)
                local = jnp.dot(jnp.concatenate(weights, 1), both, preferred_element_type=f32)
                y_s[:, lanes] = local + skip_ref[:, lanes] * pair

    early = jnp.minimum(2 + g, STEPS)
    local_chunks(0, 1)

    ka.wait_recv()
    ktb[...] = k_ref[...] * rka[...]
    kb = keep_copy(ktb, rkb, 1, x_peer)
    kb.start()
    is_core0 = c == 0
    is_x0 = x == 0

    step_b = [copy(tb.at[1 - x, d], rb.at[d], 1, j, x_peer) for j, d in enumerate(part)]
    for j, d in enumerate(part):
        step_a[j].wait_recv()
        own = s_ref[c, :, d].astype(f32)
        peer = ra[:, d].astype(f32)
        first = jnp.where(is_core0, own, peer)
        second = jnp.where(is_core0, peer, own)
        keep = jnp.where(is_core0, rka[d], k_ref[d])
        tb[:, d] = (keep[None, :, None, :] * first + second).astype(bf16)
        step_b[j].start()

    local_chunks(1, early)

    kb.wait_recv()
    step_c = [copy(sc.at[d], rc.at[d], 2, j, idx + 4) for j, d in enumerate(part)]
    step_d = [copy(sd.at[d], rd.at[d], 3, j, x_peer) for j, d in enumerate(part)]
    for j, d in enumerate(part):
        step_b[j].wait_recv()
        own = tb[x, d].astype(f32)
        peer = rb[d].astype(f32)
        first = jnp.where(is_x0, own, peer)
        second = jnp.where(is_x0, peer, own)
        keep0 = jnp.where(is_x0, ktb[d], rkb[d])[:, None, :]
        keep1 = jnp.where(is_x0, rkb[d], ktb[d])[:, None, :]

        @pl.when(has_prev)
        def _():
            step_c[j].wait_recv()

        entry = rc[d].astype(f32)
        after = keep0 * entry + first

        @pl.when(has_next)
        def _():
            sc[d] = (keep1 * after + second).astype(bf16)
            step_c[j].start()

        sd[d] = jnp.where(is_x0, after, entry).astype(bf16)
        step_d[j].start()
        oe[d] = jnp.where(is_x0, entry, after).astype(bf16)

    local_chunks(early, STEPS)
    z_load.wait()

    step_e = [copy(se.at[:, d], e_s.at[c, :, d], 4, j, core_peer) for j, d in enumerate(part)]
    squares = jnp.zeros((length, 128), f32)
    c_cols = c_ref[...]
    for j in range(STEPS + 1):
        if j < STEPS:
            d = part[j]
            step_d[j].wait_recv()
            keep = jnp.where(is_core0, k_ref[d], rka[d])[:, None, :]
            for quarter, source in ((x, oe), (1 - x, rd)):
                entry = source[d].astype(f32)
                mine = jnp.where(
                    is_core0, s_ref[c, quarter, d].astype(f32), ra[quarter, d].astype(f32)
                )
                after = keep * entry + mine
                e_s[c, quarter, d] = jnp.where(is_core0, entry, after).astype(bf16)
                se[quarter, d] = jnp.where(is_core0, after, entry).astype(bf16)
            step_e[j].start()
        if j > 0:
            i = j - 1
            step_e[i].wait_recv()
            grown = jnp.exp(cum_ref[i])
            for n in range(size // 2):
                lanes = slice(i * cols + n * 128, i * cols + (n + 1) * 128)
                entry = jnp.concatenate(
                    [
                        e_s[q // 2, q % 2, i * size + h]
                        for h in (2 * n, 2 * n + 1)
                        for q in range(4)
                    ],
                    0,
                )
                carried = jnp.dot(entry, c_cols, preferred_element_type=f32)
                carried = jnp.concatenate(
                    [
                        carried[:P_SIZE] * grown[2 * n : 2 * n + 1],
                        carried[P_SIZE:] * grown[2 * n + 1 : 2 * n + 2],
                    ],
                    0,
                ).T
                gated = (y_s[:, lanes] + carried) * silu(z_s[:, lanes].astype(f32))
                squares = squares + gated * gated
                hid_s[:, lanes] = (gated * gain_ref[:, lanes]).astype(bf16)

    sq_own[...] = lax.dot_general(
        jnp.ones((8, 128), f32), squares, (((1,), (1,)), ((), ())),
        precision=lax.Precision.HIGHEST, preferred_element_type=f32,
    )
    if chunks:
        sq_copy = pltpu.make_async_remote_copy(
            src_ref=sq_own, dst_ref=sq_s, send_sem=sq_sem.at[0], recv_sem=sq_sem.at[1],
            device_id=(idx, 1 - hd), device_id_type=MESH,
        )
        sq_copy.start()
        copies = []
        for i in range(2 * chunks):
            loads[i].wait()
            flipped = jnp.dot(hid_s[...], w_s[i], preferred_element_type=f32).T.astype(bf16)
            j = i % chunks
            rows = pl.ds(j * CHUNK, CHUNK)
            if i < chunks:
                send_s[j] = flipped
                cp = pltpu.make_async_remote_copy(
                    src_ref=send_s.at[j], dst_ref=got_ref.at[rows],
                    send_sem=psend.at[j], recv_sem=precv.at[j],
                    device_id=(idx, 1 - hd), device_id_type=MESH,
                )
                cp.start()
                copies.append(cp)
            else:
                own_ref[rows] = flipped
        sq_copy.wait()
        inv_ref[...] = lax.rsqrt((sq_own[...] + sq_s[...]) / (HEADS * P_SIZE) + EPSILON)
        for cp in copies:
            cp.wait()

    ka.wait_send()
    kb.wait_send()
    for j in range(STEPS):
        step_a[j].wait_send()
        step_b[j].wait_send()
        step_d[j].wait_send()
        step_e[j].wait_send()

    @pl.when(has_next)
    def _():
        for cp in step_c:
            cp.wait_send()


def mix(states, keep, xconv, scores, cum, delta, c_cols, skip, gain, z_in, w_out):
    heads = keep.shape[0]
    length, hid = xconv.shape
    depth, width = w_out.shape
    groups = lax.axis_size("ctx") // 4
    paired = lax.axis_size("head") == 2 and width % (2 * CHUNK) == 0
    chunks = width // 2 // CHUNK if paired else 0
    quarter = (heads,) + states.shape[3:]
    vmem = pl.BlockSpec(memory_space=pltpu.VMEM)
    bf, f32 = jnp.bfloat16, jnp.float32
    dma = pltpu.SemaphoreType.DMA
    rows8 = (8, length)
    if paired:
        half = jax.ShapeDtypeStruct((width // 2, length), bf)
        outs = [half, half, jax.ShapeDtypeStruct(rows8, f32)]
        scratch = [
            pltpu.VMEM((2 * chunks, depth, CHUNK), bf),
            pltpu.VMEM((chunks, CHUNK, length), bf),
            pltpu.VMEM(rows8, f32),
            pltpu.VMEM(rows8, f32),
            pltpu.VMEM((length, hid), bf),
            dma((2 * chunks,)),
            dma((chunks,)),
            dma((chunks,)),
            dma((2,)),
        ]
    else:
        outs = [jax.ShapeDtypeStruct((length, hid), bf), jax.ShapeDtypeStruct(rows8, f32)]
        scratch = []
    scratch += [
        pltpu.VMEM((length, hid), bf),
        dma((1,)),
        pltpu.VMEM((length, hid), f32),
        pltpu.VMEM(states.shape, bf),
        pltpu.VMEM((2,) + quarter, bf),
        pltpu.VMEM(keep.shape, f32),
        pltpu.VMEM((2,) + quarter, bf),
        pltpu.VMEM(keep.shape, f32),
        pltpu.VMEM(quarter, bf),
        pltpu.VMEM(keep.shape, f32),
    ]
    scratch += [pltpu.VMEM(quarter, bf)] * 5
    scratch += [
        pltpu.VMEM((2,) + quarter, bf),
        dma((5, STEPS)),
        dma((5, STEPS)),
        dma((2,)),
        dma((2,)),
    ]
    result = pl.pallas_call(
        functools.partial(mixer_kernel, groups, chunks),
        out_shape=outs,
        in_specs=[vmem] * 9 + [pl.BlockSpec(memory_space=pl.ANY)] * 2,
        out_specs=[vmem] * len(outs),
        scratch_shapes=scratch,
        compiler_params=pltpu.CompilerParams(
            collective_id=0, has_side_effects=True, vmem_limit_bytes=44 * 1024 * 1024
        ),
    )(states, keep, xconv, scores, cum, delta, c_cols, skip, gain, z_in, w_out)
    if not paired:
        return project_any(result[0], result[1], w_out)
    own, got, inverse = result
    total = own.astype(f32) + got.astype(f32)
    return (total * inverse[:1]).astype(bf)


def local_kernel(
    x_ref, xt_ref, bc_ref, bct_ref, dt_ref, bias_ref, rate_ref, cx_ref, cbc_ref,
    xc_ref, st_ref, keep_ref, score_ref, cum_ref, delta_ref, c_ref, b_s,
):
    f32, bf16 = jnp.float32, jnp.bfloat16
    step = pl.program_id(0)
    heads = dt_ref.shape[0]
    block = heads // STEPS
    length = x_ref.shape[0]

    @pl.when(step == 0)
    def _():
        lead = bct_ref.shape[1]
        wide = jnp.concatenate([bct_ref[...], bc_ref[...]], 1).astype(f32)
        summed = jnp.zeros(bc_ref.shape, f32)
        for k in range(KCONV):
            first = lead - KCONV + 1 + k
            summed = summed + cbc_ref[:, k : k + 1] * wide[:, first : first + length]
        bcconv = silu(summed)
        b_s[...] = bcconv[:N].astype(bf16)
        c_ref[...] = bcconv[N:].astype(bf16)
        c_rows = bcconv[N:].T.astype(bf16)
        scores = jnp.dot(c_rows, b_s[...], preferred_element_type=f32)
        rows = lax.broadcasted_iota(jnp.int32, (length, length), 0)
        cols = lax.broadcasted_iota(jnp.int32, (length, length), 1)
        score_ref[...] = jnp.where(rows >= cols, scores, 0.0)
        raw = dt_ref[...] + bias_ref[...]
        delta = jnp.maximum(raw, 0.0) + jnp.log1p(jnp.exp(-jnp.abs(raw)))
        upper = jnp.where(rows <= cols, 1.0, 0.0)
        cum = jnp.dot(
            -delta * rate_ref[...], upper,
            precision=lax.Precision.HIGHEST, preferred_element_type=f32,
        )
        keep_ref[...] = jnp.broadcast_to(jnp.exp(cum[:, length - 1 : length]), keep_ref.shape)
        for i in range(STEPS):
            part = slice(i * block, (i + 1) * block)
            cum_ref[i, 0:block] = cum[part]
            delta_ref[i, 0:block] = delta[part]

    lead = xt_ref.shape[0]
    cum8 = cum_ref[step]
    delta8 = delta_ref[step]
    tail8 = jnp.exp(cum8[:, length - 1 : length] - cum8) * delta8
    b_rows = b_s[...]
    for j in range(block // 2):
        lanes = slice(j * 128, (j + 1) * 128)
        wide = jnp.concatenate([xt_ref[:, lanes].astype(f32), x_ref[:, lanes].astype(f32)], 0)
        summed = jnp.zeros((length, 128), f32)
        for k in range(KCONV):
            first = lead - KCONV + 1 + k
            summed = summed + cx_ref[k : k + 1, lanes] * wide[first : first + length]
        pair = silu(summed).astype(bf16)
        xc_ref[:, lanes] = pair
        pair32 = pair.astype(f32)
        flipped = pair32.T
        for half in range(2):
            h = 2 * j + half
            scaled = (flipped[half * P_SIZE : (half + 1) * P_SIZE] * tail8[h : h + 1]).astype(bf16)
            state = lax.dot_general(
                scaled, b_rows, (((1,), (1,)), ((), ())), preferred_element_type=f32
            ).astype(bf16)
            for quarter in range(4):
                st_ref[quarter // 2, quarter % 2, h] = state[quarter * 16 : (quarter + 1) * 16]


def local_terms(x_in, x_tail, bc, bc_tail, dt_in, dt_bias, decay_rate, conv_x, conv_bc):
    length, width = x_in.shape
    heads = width // P_SIZE
    block = heads // STEPS
    cols = block * P_SIZE
    f32, bf16 = jnp.float32, jnp.bfloat16

    def whole(a):
        return pl.BlockSpec(a.shape, lambda i: (0,) * len(a.shape))

    def columns(rows):
        return pl.BlockSpec((rows, cols), lambda i: (0, i))

    args = (
        x_in, x_tail, bc, bc_tail, dt_in, dt_bias[:, None], decay_rate[:, None],
        conv_x, conv_bc,
    )
    in_specs = [columns(length), columns(x_tail.shape[0])] + [whole(a) for a in args[2:7]]
    in_specs += [columns(KCONV), whole(conv_bc)]
    outs = [
        jax.ShapeDtypeStruct((length, width), bf16),
        jax.ShapeDtypeStruct((2, 2, heads, P_SIZE // 4, N), bf16),
        jax.ShapeDtypeStruct((heads, N), f32),
        jax.ShapeDtypeStruct((length, length), f32),
        jax.ShapeDtypeStruct((STEPS, 8, length), f32),
        jax.ShapeDtypeStruct((STEPS, 8, length), f32),
        jax.ShapeDtypeStruct((N, length), bf16),
    ]
    out_specs = [
        columns(length),
        pl.BlockSpec((2, 2, block, P_SIZE // 4, N), lambda i: (0, 0, i, 0, 0)),
    ] + [whole(a) for a in outs[2:]]
    return pl.pallas_call(
        local_kernel,
        out_shape=outs,
        grid=(STEPS,),
        in_specs=in_specs,
        out_specs=out_specs,
        scratch_shapes=[
            pltpu.VMEM((N, length), bf16),
        ],
        compiler_params=pltpu.CompilerParams(vmem_limit_bytes=32 * 1024 * 1024),
    )(*args)


def project_any(hidden, squares, w_out):
    inverse = lax.rsqrt(lax.psum(squares[0], "head") / (HEADS * P_SIZE) + EPSILON)
    ranks = lax.axis_size("head")
    rank = lax.axis_index("head")
    share = w_out.shape[1] // ranks

    def project(owner):
        rows = lax.dynamic_slice_in_dim(w_out, owner * share, share, 1)
        return lax.dot_general(
            rows, hidden, (((0,), (1,)), ((), ())), preferred_element_type=jnp.float32
        ).astype(jnp.bfloat16)

    arrived = []
    for shift in range(1, ranks):
        piece = project(lax.rem(rank + shift, ranks))
        arrived.append(
            lax.ppermute(piece, "head", [(i, (i + shift) % ranks) for i in range(ranks)])
        )
    total = project(rank).astype(jnp.float32)
    for piece in arrived:
        total = total + piece.astype(jnp.float32)
    return (total * inverse[None, :]).astype(jnp.bfloat16)


def on_device(
    x_in, z_in, bc_in, dt_in, dt_bias, decay_rate, d_skip, conv_x, conv_bc, norm_gain, w_out
):
    tok_rows = x_in.shape[0]
    hid_cols = x_in.shape[1]
    bc = lax.all_gather(bc_in, "head", axis=0, tiled=True)
    tails = jnp.concatenate([x_in[tok_rows - 16 :].reshape(-1, 128), bc[:, tok_rows - 128 :]], 0)
    before = from_behind(tails, "ctx", 1)
    x_tail = before[: hid_cols // 8].reshape(16, hid_cols)
    bc_tail = before[hid_cols // 8 :]
    terms = local_terms(
        x_in, x_tail, bc, bc_tail, dt_in, dt_bias, decay_rate, conv_x, conv_bc
    )
    xconv, states, keep, scores, cum, delta, c_cols = terms
    skip = jnp.repeat(d_skip, P_SIZE)[None, :]
    return mix(
        states, keep, xconv, scores, cum, delta, c_cols, skip, norm_gain[None, :], z_in, w_out
    )


def solution(mesh):
    in_specs = (
        P("ctx", "head"),
        P("ctx", "head"),
        P("head", "ctx"),
        P("head", "ctx"),
        P("head"),
        P("head"),
        P("head"),
        P(None, "head"),
        P(),
        P("head"),
        P("head", None),
    )
    out_specs = P("head", "ctx")
    return jax.shard_map(
        on_device, mesh=mesh, in_specs=in_specs, out_specs=out_specs, check_vma=False
    )
```

profile of v0, /device:TPU:25, one launch (start us, length us, event | category | flops | bytes accessed | tf_op | source)
XLA Modules:
  0.0 60.5 jit_solution(2598917096679981400)
XLA Ops:
  0.0 0.0 copy-start
  0.0 0.0 copy-start.3
  0.0 0.0 copy-start.2
  0.0 1.0 %slice.15 = bf16[16,2560]{1,0:T(8,128)(2,1)S(1)} slice(bf16[256,2560]{1,0:T(8,128)(2,1)} %x_ref.1), slice={[240:256], [0:2560]} | slice | bytes 163840 | tf_op jit(solution)/shard_map/slice | solution.py:483
  1.0 0.1 reshape.6
  1.1 4.0 %all_gather.3.bc_ref = bf16[256,256]{1,0:T(8,128)(2,1)S(1)} all-gather(bf16[128,256]{1,0:T(8,128)(2,1)} %param.13), channel_id=1, replica_groups=mesh['ctx'=16,'head'=2] {'head'}, dimensions={0}, use_global_device_ids=true | all-gather | bytes 196608 | tf_op jit(solution)/shard_map/all_gather | solution.py:482
  5.2 0.0 copy-start.1
  5.2 5.0 %collective-permute-start = (bf16[576,128]{1,0:T(8,128)(2,1)S(1)}, bf16[576,128]{1,0:T(8,128)(2,1)S(1)}, u32[]{:S(2)}, u32[]{:S(2)}) collective-permute-start(bf16[576,128]{1,0:T(8,128)(2,1)S(1)} %pad_maximum_fusion), channel_id=1, source_target_pairs={{0,2},{2,4},{4,6},{6,8},{8,10},{10,12},{12,14},{14,16},{16,18},{18... | collective-permute-start | bytes 442376 | tf_op jit(solution)/shard_map/ppermute | solution.py:24
  10.1 0.7 %broadcast_in_dim.15.gain_ref = f32[1,2560]{1,0:T(1,128)S(1)} reshape(f32[2560]{0:T(1024)} %param.20) | data formatting | bytes 20480 | tf_op jit(solution)/shard_map/broadcast_in_dim | solution.py:493
  10.9 0.7 %copy.12.bias_ref = f32[40,1]{1,0:T(8,128)S(1)} copy(f32[40,1]{0,1:T(1,128)} %bitcast.4) | data formatting | bytes 320 | tf_op jit(solution)/shard_map/broadcast_in_dim | solution.py:422
  11.6 0.7 %copy.13.rate_ref = f32[40,1]{1,0:T(8,128)S(1)} copy(f32[40,1]{0,1:T(1,128)} %bitcast.5) | data formatting | bytes 320 | tf_op jit(solution)/shard_map/broadcast_in_dim | solution.py:422
  12.3 0.7 %broadcast_in_dim.14 = f32[40,64]{1,0:T(8,128)S(1)} broadcast(f32[40]{0:T(128)} %param.17), dimensions={0} | broadcast | bytes 10400 | tf_op jit(solution)/shard_map/broadcast_in_dim | solution.py:491
  13.1 0.1 broadcast_in_dim_reshape.3.skip_ref
  13.2 0.8 %copy.14.cbc_ref = f32[256,4]{1,0:T(8,128)S(1)} copy(f32[256,4]{0,1:T(4,128)} %param.19) | data formatting | bytes 8192 | tf_op args[8]
  14.0 0.0 collective-permute-done
  14.0 0.1 reshape.7.xt_ref
  14.1 0.0 copy-done
  14.2 0.0 copy-done.3
  14.2 0.0 copy-done.2
  14.2 5.5 %shard_map.109 = (bf16[256,2560]{1,0:T(8,128)(2,1)S(1)}, bf16[2,2,40,16,128]{4,3,2,1,0:T(8,128)(2,1)S(1)}, f32[40,128]{1,0:T(8,128)S(1)}, f32[256,256]{1,0:T(8,1...) custom-call(bf16[256,2560]{1,0:T(8,128)(2,1)S(1)} %copy-done, ...), custom_call_target="tpu_custom_call" | custom-call | tf_op jit(solution)/shard_map/pallas_call | solution.py:440
  19.7 0.0 copy-done.1
  19.7 39.7 %shard_map.110 = (bf16[1280,256]{1,0:T(8,128)(2,1)S(1)}, bf16[1280,256]{1,0:T(8,128)(2,1)S(1)}, f32[8,256]{1,0:T(8,128)S(1)}) custom-call(bf16[2,2,40,16,128]{4,3,2,1,0:T(8,128)(2,1)S(1)} %get-tuple-element.15.s_ref, f32[40,128]{1,0:T(8,128)S(1)} %get-tuple-element.16.k_ref, bf16[256,2560]{1,0:T(8,128)(2,1)S(1)} %get-tuple-element.17.xc_ref, ...), custom_call_target="tpu_custom_call" | custom-call | tf_op jit(solution)/shard_map/pallas_call | solution.py:326
  59.4 1.0 %multiply_convert_fusion = bf16[1280,256]{1,0:T(8,128)(2,1)} fusion(bf16[1280,256]{1,0:T(8,128)(2,1)S(1)} %get-tuple-element.23, bf16[1280,256]{1,0:T(8,128)(2,1)S(1)} %get-tuple-element.22, f32[256]{0:T(256)S(1)} %bitcast.3), kind=kLoop, calls=%fused_computation | loop fusion | flops 1638400 | bytes 1967104 | tf_op jit(solution)/shard_map/convert_element_type | solution.py:340
  (5 shorter events, 0.0 us)
Async XLA Ops:
  0.0 14.1 %copy-start = (bf16[256,2560]{1,0:T(8,128)(2,1)S(1)}, bf16[256,2560]{1,0:T(8,128)(2,1)}, u32[]{:S(2)}) copy-start(bf16[256,2560]{1,0:T(8,128)(2,1)} %x_ref.1) | copy-start | bytes 3932164
  0.0 14.1 %copy-start.3 = (f32[4,2560]{1,0:T(4,128)S(1)}, f32[4,2560]{1,0:T(4,128)}, u32[]{:S(2)}) copy-start(f32[4,2560]{1,0:T(4,128)} %cx_ref.1) | copy-start | bytes 122884
  0.0 14.2 %copy-start.2 = (f32[40,256]{1,0:T(8,128)S(1)}, f32[40,256]{1,0:T(8,128)}, u32[]{:S(2)}) copy-start(f32[40,256]{1,0:T(8,128)} %dt_ref.1) | copy-start | bytes 122884
  5.2 14.6 %copy-start.1 = (bf16[256,2560]{1,0:T(8,128)(2,1)S(1)}, bf16[256,2560]{1,0:T(8,128)(2,1)}, u32[]{:S(2)}) copy-start(bf16[256,2560]{1,0:T(8,128)(2,1)} %z_ref.1) | copy-start | bytes 3932164
  5.2 8.8 %collective-permute-start = (bf16[576,128]{1,0:T(8,128)(2,1)S(1)}, bf16[576,128]{1,0:T(8,128)(2,1)S(1)}, u32[]{:S(2)}, u32[]{:S(2)}) collective-permute-start(bf16[576,128]{1,0:T(8,128)(2,1)S(1)} %pad_maximum_fusion), channel_id=1, source_target_pairs={{0,2},{2,4},{4,6},{6,8},{8,10},{10,12},{12,14},{14,16},{16,18},{18... | collective-permute-start | bytes 442376 | tf_op jit(solution)/shard_map/ppermute | solution.py:24
where the time goes:
time: 60.8 us; the launch traced here: 60.5 us
  Pallas kernels  45.2 us (74%)
  local copies, waits for them, and re-layouts  5.1 us (8%)
  starting transfers between devices  4.96 us (8%)
  blocking collectives  4 us (7%)
  other arithmetic  1.06 us (2%)
    pallas_call x1, Pallas kernels, mix(): pl.pallas_call(functools.partial(mixer_kernel, groups, chunks), out_shape...  39.7 us
    pallas_call x1, Pallas kernels, local_terms(): pl.pallas_call(local_kernel, out_shape=outs, grid=(STEPS,), in_specs=in_s...  5.55 us
    ppermute x1, starting transfers between devices, from_behind(): lax.ppermute(value, axis, [(source, source + steps) for source in range(f...  4.96 us
    all_gather x1, blocking collectives, on_device(): bc = lax.all_gather(bc_in, 'head', axis=0, tiled=True)  4 us
  transfers between devices with their start and end apart: 1, of which 0 were waited for; matrix products, arithmetic and copies ran while one was open for 6% of the time, Pallas kernels for 0%

commit v1 on v0

--- a/solution.py
+++ b/solution.py
@@ -16,12 +16,6 @@
 
 EPSILON = 1e-05
 MESH = pl.DeviceIdType.MESH
-
-
-def from_behind(value, axis, steps):
-    count = lax.axis_size(axis)
-    first, last = (max(0, -steps), min(count, count - steps))
-    return lax.ppermute(value, axis, [(source, source + steps) for source in range(first, last)])
 
 
 STEPS = 5
@@ -129,7 +123,8 @@
                     [jnp.where(left, pair, 0.0), jnp.where(left, 0.0, pair)], 0
                 ).astype(bf16)
                 local = jnp.dot(jnp.concatenate(weights, 1), both, preferred_element_type=f32)
-                y_s[:, lanes] = local + skip_ref[:, lanes] * pair
+                first = i * size + 2 * j
+                y_s[:, lanes] = local + jnp.where(left, skip_ref[first], skip_ref[first + 1]) * pair
 
     early = jnp.minimum(2 + g, STEPS)
     local_chunks(0, 1)
@@ -226,7 +221,7 @@
                 ).T
                 gated = (y_s[:, lanes] + carried) * silu(z_s[:, lanes].astype(f32))
                 squares = squares + gated * gated
-                hid_s[:, lanes] = (gated * gain_ref[:, lanes]).astype(bf16)
+                hid_s[:, lanes] = (gated * gain_ref[lanes][None, :]).astype(bf16)
 
     sq_own[...] = lax.dot_general(
         jnp.ones((8, 128), f32), squares, (((1,), (1,)), ((), ())),
@@ -326,7 +321,9 @@
     result = pl.pallas_call(
         functools.partial(mixer_kernel, groups, chunks),
         out_shape=outs,
-        in_specs=[vmem] * 9 + [pl.BlockSpec(memory_space=pl.ANY)] * 2,
+        in_specs=[vmem] * 7
+        + [pl.BlockSpec(memory_space=pltpu.SMEM), vmem]
+        + [pl.BlockSpec(memory_space=pl.ANY)] * 2,
         out_specs=[vmem] * len(outs),
         scratch_shapes=scratch,
         compiler_params=pltpu.CompilerParams(
@@ -340,6 +337,104 @@
     return (total * inverse[:1]).astype(bf)
 
 
+def rim_kernel(count, ranks, bc_ref, x_ref, all_ref, bct_ref, xt_ref, send, recv):
+    idx = lax.axis_index("ctx")
+    hd = lax.axis_index("head")
+    has_prev = idx > 0
+    has_next = idx < count - 1
+    rows, length = bc_ref.shape
+    lead = xt_ref.shape[0]
+    barrier = pltpu.get_barrier_semaphore()
+
+    def greet(place, shift):
+        other = lax.rem(hd + shift, ranks)
+        pl.semaphore_signal(barrier, inc=1, device_id=(place, other), device_id_type=MESH)
+
+    for shift in range(1, ranks):
+        greet(idx, shift)
+
+    @pl.when(has_prev)
+    def _():
+        for shift in range(ranks):
+            greet(idx - 1, shift)
+
+    @pl.when(has_next)
+    def _():
+        for shift in range(ranks):
+            greet(idx + 1, shift)
+
+    mine = pl.ds(pl.multiple_of(hd * rows, rows), rows)
+    all_ref[mine] = bc_ref[...]
+
+    @pl.when(jnp.logical_not(has_prev))
+    def _():
+        bct_ref[...] = jnp.zeros_like(bct_ref)
+        xt_ref[...] = jnp.zeros_like(xt_ref)
+
+    neighbours = has_prev.astype(jnp.int32) + has_next.astype(jnp.int32)
+    pl.semaphore_wait(barrier, ranks - 1 + ranks * neighbours)
+
+    def copy(src, dst, kind, shift, place):
+        return pltpu.make_async_remote_copy(
+            src_ref=src, dst_ref=dst, send_sem=send.at[kind, shift], recv_sem=recv.at[kind, shift],
+            device_id=(place, lax.rem(hd + shift, ranks)), device_id_type=MESH,
+        )
+
+    across = [copy(bc_ref, all_ref.at[mine], 0, k, idx) for k in range(1, ranks)]
+    ahead = [copy(x_ref.at[pl.ds(x_ref.shape[0] - lead, lead)], xt_ref, 2, 0, idx + 1)]
+    last = bc_ref.at[:, pl.ds(length - 128, 128)]
+    ahead += [copy(last, bct_ref.at[mine], 1, k, idx + 1) for k in range(ranks)]
+
+    @pl.when(has_next)
+    def _():
+        for cp in ahead:
+            cp.start()
+
+    for cp in across:
+        cp.start()
+
+    @pl.when(has_prev)
+    def _():
+        for cp in ahead:
+            cp.wait_recv()
+
+    for cp in across:
+        cp.wait()
+
+    @pl.when(has_next)
+    def _():
+        for cp in ahead:
+            cp.wait_send()
+
+
+def with_rims(bc_in, x_in):
+    rows, length = bc_in.shape
+    ranks = lax.axis_size("head")
+    vmem = pl.BlockSpec(memory_space=pltpu.VMEM)
+    dtype = bc_in.dtype
+    return pl.pallas_call(
+        functools.partial(rim_kernel, lax.axis_size("ctx"), ranks),
+        out_shape=[
+            jax.ShapeDtypeStruct((rows * ranks, length), dtype),
+            jax.ShapeDtypeStruct((rows * ranks, 128), dtype),
+            jax.ShapeDtypeStruct((16, x_in.shape[1]), dtype),
+        ],
+        in_specs=[vmem, pl.BlockSpec(memory_space=pl.ANY)],
+        out_specs=[vmem] * 3,
+        scratch_shapes=[pltpu.SemaphoreType.DMA((3, ranks)), pltpu.SemaphoreType.DMA((3, ranks))],
+        compiler_params=pltpu.CompilerParams(
+            collective_id=1, has_side_effects=True, vmem_limit_bytes=8 * 1024 * 1024
+        ),
+    )(bc_in, x_in)
+
+
+def as_column(row):
+    size = row.shape[0]
+    rows = lax.broadcasted_iota(jnp.int32, (size, size), 0)
+    cols = lax.broadcasted_iota(jnp.int32, (size, size), 1)
+    return jnp.sum(jnp.where(rows == cols, row[None, :], 0.0), axis=1, keepdims=True)
+
+
 def local_kernel(
     x_ref, xt_ref, bc_ref, bct_ref, dt_ref, bias_ref, rate_ref, cx_ref, cbc_ref,
     xc_ref, st_ref, keep_ref, score_ref, cum_ref, delta_ref, c_ref, b_s,
@@ -355,9 +450,10 @@
         lead = bct_ref.shape[1]
         wide = jnp.concatenate([bct_ref[...], bc_ref[...]], 1).astype(f32)
         summed = jnp.zeros(bc_ref.shape, f32)
+        taps = jnp.concatenate([cbc_ref[...], jnp.zeros_like(cbc_ref)], 0).T
         for k in range(KCONV):
             first = lead - KCONV + 1 + k
-            summed = summed + cbc_ref[:, k : k + 1] * wide[:, first : first + length]
+            summed = summed + taps[:, k : k + 1] * wide[:, first : first + length]
         bcconv = silu(summed)
         b_s[...] = bcconv[:N].astype(bf16)
         c_ref[...] = bcconv[N:].astype(bf16)
@@ -366,11 +462,11 @@
         rows = lax.broadcasted_iota(jnp.int32, (length, length), 0)
         cols = lax.broadcasted_iota(jnp.int32, (length, length), 1)
         score_ref[...] = jnp.where(rows >= cols, scores, 0.0)
-        raw = dt_ref[...] + bias_ref[...]
+        raw = dt_ref[...] + as_column(bias_ref[...])
         delta = jnp.maximum(raw, 0.0) + jnp.log1p(jnp.exp(-jnp.abs(raw)))
         upper = jnp.where(rows <= cols, 1.0, 0.0)
         cum = jnp.dot(
-            -delta * rate_ref[...], upper,
+            -delta * as_column(rate_ref[...]), upper,
             precision=lax.Precision.HIGHEST, preferred_element_type=f32,
         )
         keep_ref[...] = jnp.broadcast_to(jnp.exp(cum[:, length - 1 : length]), keep_ref.shape)
@@ -419,11 +515,11 @@
         return pl.BlockSpec((rows, cols), lambda i: (0, i))
 
     args = (
-        x_in, x_tail, bc, bc_tail, dt_in, dt_bias[:, None], decay_rate[:, None],
-        conv_x, conv_bc,
+        x_in, x_tail, bc, bc_tail, dt_in, dt_bias, decay_rate,
+        conv_x, conv_bc.T,
     )
     in_specs = [columns(length), columns(x_tail.shape[0])] + [whole(a) for a in args[2:7]]
-    in_specs += [columns(KCONV), whole(conv_bc)]
+    in_specs += [columns(KCONV), whole(args[8])]
     outs = [
         jax.ShapeDtypeStruct((length, width), bf16),
         jax.ShapeDtypeStruct((2, 2, heads, P_SIZE // 4, N), bf16),
@@ -477,20 +573,13 @@
 def on_device(
     x_in, z_in, bc_in, dt_in, dt_bias, decay_rate, d_skip, conv_x, conv_bc, norm_gain, w_out
 ):
-    tok_rows = x_in.shape[0]
-    hid_cols = x_in.shape[1]
-    bc = lax.all_gather(bc_in, "head", axis=0, tiled=True)
-    tails = jnp.concatenate([x_in[tok_rows - 16 :].reshape(-1, 128), bc[:, tok_rows - 128 :]], 0)
-    before = from_behind(tails, "ctx", 1)
-    x_tail = before[: hid_cols // 8].reshape(16, hid_cols)
-    bc_tail = before[hid_cols // 8 :]
+    bc, bc_tail, x_tail = with_rims(bc_in, x_in)
     terms = local_terms(
         x_in, x_tail, bc, bc_tail, dt_in, dt_bias, decay_rate, conv_x, conv_bc
     )
     xconv, states, keep, scores, cum, delta, c_cols = terms
-    skip = jnp.repeat(d_skip, P_SIZE)[None, :]
     return mix(
-        states, keep, xconv, scores, cum, delta, c_cols, skip, norm_gain[None, :], z_in, w_out
+        states, keep, xconv, scores, cum, delta, c_cols, d_skip, norm_gain, z_in, w_out
     )
 
 

time: 60.8 us -> 58.5 us (0.962)
  Pallas kernels: 45.2 us -> 52.6 us
  starting transfers between devices: 4.96 us -> 0 us
  blocking collectives: 4 us -> 0 us
  local copies, waits for them, and re-layouts: 5.1 us -> 4.45 us
    pallas_call x0 -> x1, Pallas kernels: none -> 5.77 us  [with_rims(): pl.pallas_call(functools.partial(rim_kernel, lax.axis_size('ctx'), ranks)...]
    ppermute x1 -> x0, starting transfers between devices: 4.96 us -> none  [from_behind(): lax.ppermute(value, axis, [(source, source + steps) for source in range(f...]
    all_gather x1 -> x0, blocking collectives: 4 us -> none  [on_device(): bc = lax.all_gather(bc_in, 'head', axis=0, tiled=True)]
    unnamed x9 -> x22, local copies, waits for them, and re-layouts: 0.83 us -> 4.45 us
    broadcast_in_dim x4 -> x0, local copies, waits for them, and re-layouts: 2.92 us -> none  [the longest x1 0.74 us: local_terms(): dt_bias[:, None]]
    pallas_call x1, Pallas kernels: 39.7 us -> 41.1 us  [mix(): pl.pallas_call(functools.partial(mixer_kernel, groups, chunks), out_shape...]
    slice x4 -> x0, local copies, waits for them, and re-layouts: 1.02 us -> none  [the longest x1 1 us: on_device(): x_in[tok_rows - 16:].reshape(-1, 128)]
  transfers between devices with their start and end apart: 1 -> 0, of which waited for: 0 -> 0; matrix products, arithmetic and copies ran while one was open for 6% -> 0% of each run, Pallas kernels for 0% -> 0%
where the time goes in v1:
time: 58.5 us; the launch traced here: 58.1 us
  Pallas kernels  52.6 us (90%)
  local copies, waits for them, and re-layouts  4.45 us (8%)
  other arithmetic  1.04 us (2%)
    pallas_call x1, Pallas kernels, mix(): pl.pallas_call(functools.partial(mixer_kernel, groups, chunks), out_shape...  41.1 us
    pallas_call x1, Pallas kernels, with_rims(): pl.pallas_call(functools.partial(rim_kernel, lax.axis_size('ctx'), ranks)...  5.77 us
    pallas_call x1, Pallas kernels, local_terms(): pl.pallas_call(local_kernel, out_shape=outs, grid=(STEPS,), in_specs=in_s...  5.67 us
    unnamed x22, local copies, waits for them, and re-layouts  4.45 us

profile of v1, /device:TPU:25, one launch (start us, length us, event | category | flops | bytes accessed | tf_op | source)
XLA Modules:
  0.0 58.1 jit_solution(17399024475280584972)
XLA Ops:
  0.0 0.0 copy-start.9
  0.0 0.0 copy-start.8
  0.0 0.0 copy-start.10
  0.0 0.0 copy-start
  0.0 1.3 %copy-done = bf16[256,2560]{1,0:T(8,128)(2,1)S(1)} copy-done((bf16[256,2560]{1,0:T(8,128)(2,1)S(1)}, bf16[256,2560]{1,0:T(8,128)(2,1)}, u32[]{:S(2)}) %copy-start) | copy-done | bytes 1310744
  1.4 0.0 copy-start.3
  1.4 0.8 %copy-done.3 = bf16[128,256]{1,0:T(8,128)(2,1)S(1)} copy-done((bf16[128,256]{1,0:T(8,128)(2,1)S(1)}, bf16[128,256]{1,0:T(8,128)(2,1)}, u32[]{:S(2)}) %copy-start.3) | copy-done | bytes 65560
  2.2 0.0 copy-start.1
  2.2 0.0 copy-start.2
  2.2 5.8 %shard_map.109 = (bf16[256,256]{1,0:T(8,128)(2,1)S(1)}, bf16[256,128]{1,0:T(8,128)(2,1)S(1)}, bf16[16,2560]{1,0:T(8,128)(2,1)S(1)}) custom-call(bf16[128,256]{1,0:T(8,128)(2,1)S(1)} %copy-done.3, bf16[256,2560]{1,0:T(8,128)(2,1)S(1)} %copy-done), custom_call_target="tpu_custom_call" | custom-call | tf_op jit(solution)/shard_map/pallas_call | solution.py:415
  8.0 0.0 copy-done.9
  8.0 0.0 copy-done.8
  8.0 0.0 copy-done.1
  8.0 0.0 copy-start.4
  8.0 0.8 %copy-done.4 = f32[40,256]{1,0:T(8,128)S(1)} copy-done((f32[40,256]{1,0:T(8,128)S(1)}, f32[40,256]{1,0:T(8,128)}, u32[]{:S(2)}) %copy-start.4) | copy-done | bytes 40984
  8.8 0.0 copy-start.5
  8.8 0.8 %copy-done.5 = f32[4,2560]{1,0:T(4,128)S(1)} copy-done((f32[4,2560]{1,0:T(4,128)S(1)}, f32[4,2560]{1,0:T(4,128)}, u32[]{:S(2)}) %copy-start.5) | copy-done | bytes 40984
  9.6 0.7 %copy-done.7 = f32[256,4]{0,1:T(4,128)S(1)} copy-done((f32[256,4]{0,1:T(4,128)S(1)}, f32[256,4]{0,1:T(4,128)}, u32[]{:S(2)}) %copy-start.7) | copy-done | bytes 4120
  10.3 5.7 %shard_map.110 = (bf16[256,2560]{1,0:T(8,128)(2,1)S(1)}, bf16[2,2,40,16,128]{4,3,2,1,0:T(8,128)(2,1)S(1)}, f32[40,128]{1,0:T(8,128)S(1)}, f32[256,256]{1,0:T(8,1...) custom-call(bf16[256,2560]{1,0:T(8,128)(2,1)S(1)} %copy-done.1, ...), custom_call_target="tpu_custom_call" | custom-call | tf_op jit(solution)/shard_map/pallas_call | solution.py:536
  15.9 0.0 copy-done.10
  16.0 0.0 copy-done.2
  16.0 0.0 copy-done.6
  16.0 41.1 %shard_map.111 = (bf16[1280,256]{1,0:T(8,128)(2,1)S(1)}, bf16[1280,256]{1,0:T(8,128)(2,1)S(1)}, f32[8,256]{1,0:T(8,128)S(1)}) custom-call(bf16[2,2,40,16,128]{4,3,2,1,0:T(8,128)(2,1)S(1)} %get-tuple-element.21.s_ref, f32[40,128]{1,0:T(8,128)S(1)} %get-tuple-element.22.k_ref, bf16[256,2560]{1,0:T(8,128)(2,1)S(1)} %get-tuple-element.23.xc_ref, ...), custom_call_target="tpu_custom_call" | custom-call | tf_op jit(solution)/shard_map/pallas_call | solution.py:321
  57.1 1.0 %multiply_convert_fusion = bf16[1280,256]{1,0:T(8,128)(2,1)} fusion(bf16[1280,256]{1,0:T(8,128)(2,1)S(1)} %get-tuple-element.29, bf16[1280,256]{1,0:T(8,128)(2,1)S(1)} %get-tuple-element.28, f32[256]{0:T(256)S(1)} %bitcast.3), kind=kLoop, calls=%fused_computation | loop fusion | flops 1638400 | bytes 1967104 | tf_op jit(solution)/shard_map/convert_element_type | solution.py:337
  (3 shorter events, 0.0 us)
Async XLA Ops:
  0.0 8.0 %copy-start.9 = (f32[40]{0:T(128)S(1)}, f32[40]{0:T(128)}, u32[]{:S(2)}) copy-start(f32[40]{0:T(128)} %rate_ref.1) | copy-start | bytes 484
  0.0 8.0 %copy-start.8 = (f32[40]{0:T(128)S(1)}, f32[40]{0:T(128)}, u32[]{:S(2)}) copy-start(f32[40]{0:T(128)} %bias_ref.1) | copy-start | bytes 484
  0.0 15.9 %copy-start.10 = (f32[40]{0:T(128)S(1)}, f32[40]{0:T(128)}, u32[]{:S(2)}) copy-start(f32[40]{0:T(128)} %skip_ref.1) | copy-start | bytes 484
  0.0 1.4 %copy-start = (bf16[256,2560]{1,0:T(8,128)(2,1)S(1)}, bf16[256,2560]{1,0:T(8,128)(2,1)}, u32[]{:S(2)}) copy-start(bf16[256,2560]{1,0:T(8,128)(2,1)} %x_ref.3) | copy-start | bytes 3932164
  1.4 0.8 %copy-start.3 = (bf16[128,256]{1,0:T(8,128)(2,1)S(1)}, bf16[128,256]{1,0:T(8,128)(2,1)}, u32[]{:S(2)}) copy-start(bf16[128,256]{1,0:T(8,128)(2,1)} %bc_ref.1) | copy-start | bytes 196612
  2.2 5.8 %copy-start.1 = (bf16[256,2560]{1,0:T(8,128)(2,1)S(1)}, bf16[256,2560]{1,0:T(8,128)(2,1)}, u32[]{:S(2)}) copy-start(bf16[256,2560]{1,0:T(8,128)(2,1)} %x_ref.3) | copy-start | bytes 3932164
  2.2 13.8 %copy-start.2 = (bf16[256,2560]{1,0:T(8,128)(2,1)S(1)}, bf16[256,2560]{1,0:T(8,128)(2,1)}, u32[]{:S(2)}) copy-start(bf16[256,2560]{1,0:T(8,128)(2,1)} %z_ref.1) | copy-start | bytes 3932164
  8.0 0.8 %copy-start.4 = (f32[40,256]{1,0:T(8,128)S(1)}, f32[40,256]{1,0:T(8,128)}, u32[]{:S(2)}) copy-start(f32[40,256]{1,0:T(8,128)} %dt_ref.1) | copy-start | bytes 122884
  8.8 0.8 %copy-start.5 = (f32[4,2560]{1,0:T(4,128)S(1)}, f32[4,2560]{1,0:T(4,128)}, u32[]{:S(2)}) copy-start(f32[4,2560]{1,0:T(4,128)} %cx_ref.1) | copy-start | bytes 122884
  9.6 0.7 %copy-start.7 = (f32[256,4]{0,1:T(4,128)S(1)}, f32[256,4]{0,1:T(4,128)}, u32[]{:S(2)}) copy-start(f32[256,4]{0,1:T(4,128)} %param.19) | copy-start | bytes 12292
  10.3 5.7 %copy-start.6 = (f32[2560]{0:T(1024)S(1)}, f32[2560]{0:T(1024)}, u32[]{:S(2)}) copy-start(f32[2560]{0:T(1024)} %gain_ref.1) | copy-start | bytes 30724
